TPU v7x, 32 devices: a whole 2x2x4 slice. The times are simulated.
32 devices in a mesh: ty: 8 (over z, y), tx: 4 (over x, core).
Axes of the slice: x: 2, y: 2, z: 4, core: 2. Of those that a mesh axis runs over, the one named last changes fastest.
Arguments:
- object_field: float32 [3, 2, 1024, 512], P(None, None, 'ty', 'tx'), may hold values from -6 to 6
- probe: float32 [2, 256, 256], replicated, may hold values from -6 to 6
- propagator_phase: float32 [256, 256], replicated, may hold values from -3.140625 to 3.140625
- patterns: float32 [8, 4, 1, 256, 256], P('ty', 'tx'), may hold values from 0 to 2
- scan_positions: int32 [8, 4, 1, 2], P('ty', 'tx'), may hold values from 0 to 255
Outputs:
- updated_object: float32 [3, 2, 1024, 512], P(None, None, 'ty', 'tx')
All inputs are finite; a program needn't handle non-finite values.
Results may differ from a plain program's by a relative error of at most 0.0003.
Values sent between devices are 32-bit elements; how exact they have to be, the bound alone decides.
A program may use at most 64 MiB of HBM per device.

v0:
```python
import functools

import jax
import jax.numpy as jnp
import ml_dtypes
import numpy as np
from jax import lax
from jax.experimental import pallas as pl
from jax.experimental.pallas import tpu as pltpu
from jax.sharding import PartitionSpec as P

STEPS = 2

step_size = 0.05


def dft_tables(n):
    h = n // 2
    place = np.arange(h)
    tables = []
    for parity in (0, 1):
        turns = ((2 * place[:, None] + parity) * place[None, :]) % n
        angle = turns * (2.0 * np.pi / n)
        c = np.cos(angle) / np.sqrt(n)
        s = -np.sin(angle) / np.sqrt(n)
        block = np.block([[c, -s], [s, c]])
        for full in (block, block.T):
            high = full.astype(ml_dtypes.bfloat16)
            low = (full - high.astype(np.float64)).astype(ml_dtypes.bfloat16)
            tables += [high, low]
    return np.stack(tables)


def split2(x):
    high = x.astype(jnp.bfloat16)
    low = (x - high.astype(jnp.float32)).astype(jnp.bfloat16)
    return high, low


def split3(x):
    high = x.astype(jnp.bfloat16)
    rest = x - high.astype(jnp.float32)
    middle = rest.astype(jnp.bfloat16)
    low = (rest - middle.astype(jnp.float32)).astype(jnp.bfloat16)
    return high, middle, low


def dot(a, b):
    return jnp.dot(a, b, preferred_element_type=jnp.float32)


def cat(parts, axis):
    return jnp.concatenate(parts, axis=axis)


def cmul(a, b):
    return (a[0] * b[0] - a[1] * b[1], a[0] * b[1] + a[1] * b[0])


def cmul_conj(a, b):
    return (a[0] * b[0] + a[1] * b[1], a[0] * b[1] - a[1] * b[0])


def sin_cos(x):
    y = x * 0.5
    z = y * y
    s = jnp.float32(-2.50521083854417e-08)
    for c in (2.75573192239859e-06, -1.98412698412698e-04, 8.33333333333333e-03, -1.66666666666667e-01):
        s = s * z + jnp.float32(c)
    s = s * z * y + y
    c0 = jnp.float32(2.08767569878681e-09)
    for c in (-2.75573192239859e-07, 2.48015873015873e-05, -1.38888888888889e-03, 4.16666666666667e-02, -0.5):
        c0 = c0 * z + jnp.float32(c)
    c0 = c0 * z + 1.0
    return 2.0 * s * c0, 1.0 - 2.0 * s * s


def kernel(
    pos_ref, obj_ref, probe_ref, phase_ref, pat_ref, tab_ref, out_ref,
    tile, lit, hk, pat, wave, grad, rim, sendx, recvx, recvy, recvl,
    sem_s, sem_r,
):
    slices = obj_ref.shape[0]
    core = obj_ref.shape[2]
    n = probe_ref.shape[1]
    h = n // 2
    m = (n - core) // 2
    ty, tx = lax.axis_index("ty"), lax.axis_index("tx")
    ny, nx = lax.axis_size("ty"), lax.axis_size("tx")
    near = {
        "ty": ((ty > 0, (ty - 1, tx)), (ty < ny - 1, (ty + 1, tx))),
        "tx": ((tx > 0, (ty, tx - 1)), (tx < nx - 1, (ty, tx + 1))),
    }
    pending = []

    def copy_of(axis, side, src, dst, slot):
        return pltpu.make_async_remote_copy(
            src_ref=src, dst_ref=dst,
            send_sem=sem_s.at[slot], recv_sem=sem_r.at[slot],
            device_id=near[axis][side][1], device_id_type=pl.DeviceIdType.MESH,
        )

    def send(axis, side, src, dst, slot):
        @pl.when(near[axis][side][0])
        def _():
            copy_of(axis, side, src, dst, slot).start()

        pending.append((axis, side, src, dst, slot))

    def arrive(axis, side, src, dst, slot):
        @pl.when(near[axis][1 - side][0])
        def _():
            copy_of(axis, 1 - side, src, dst, slot).wait_recv()

    def slot_of(phase, layer, side):
        return (phase * slices + layer) * 2 + side

    barrier = pltpu.get_barrier_semaphore()
    count = jnp.int32(0)
    for axis in ("ty", "tx"):
        for there, device in near[axis]:
            @pl.when(there)
            def _():
                pl.semaphore_signal(barrier, inc=1, device_id=device, device_id_type=pl.DeviceIdType.MESH)
            count = count + there.astype(jnp.int32)
    pl.semaphore_wait(barrier, count)

    after, before = pl.ds(core, m), pl.ds(core + m, m)
    head, tail = pl.ds(0, m), pl.ds(core - m, m)
    own = pl.ds(0, core)
    other = pl.ds(core, core)

    def rim_rows(layer):
        return (
            (obj_ref.at[layer, :, head, :], tile.at[layer, :, after, own]),
            (obj_ref.at[layer, :, tail, :], tile.at[layer, :, before, own]),
        )

    for layer in range(slices):
        for side in (0, 1):
            src, dst = rim_rows(layer)[side]
            send("ty", side, src, dst, slot_of(0, layer, side))

    tile[:, :, own, own] = obj_ref[...]

    @pl.when(ty == 0)
    def _():
        tile[:, :, before, own] = jnp.zeros((slices, 2, m, core), jnp.float32)
        recvy[:, 1] = jnp.zeros(recvy.shape[:1] + recvy.shape[2:], jnp.float32)
        recvl[:, 1] = jnp.zeros(recvl.shape[:1] + recvl.shape[2:], jnp.float32)

    @pl.when(ty == ny - 1)
    def _():
        tile[:, :, after, own] = jnp.zeros((slices, 2, m, core), jnp.float32)
        recvy[:, 0] = jnp.zeros(recvy.shape[:1] + recvy.shape[2:], jnp.float32)
        recvl[:, 0] = jnp.zeros(recvl.shape[:1] + recvl.shape[2:], jnp.float32)

    @pl.when(tx == 0)
    def _():
        for phase in range(recvx.shape[0]):
            recvx[phase, :, 1] = jnp.zeros(recvx.shape[1:2] + recvx.shape[3:], jnp.float32)

    @pl.when(tx == nx - 1)
    def _():
        for phase in range(recvx.shape[0]):
            recvx[phase, :, 0] = jnp.zeros(recvx.shape[1:2] + recvx.shape[3:], jnp.float32)

    first_half = lax.broadcasted_iota(jnp.int32, (h, core), 1) < m

    def turn(x):
        return pltpu.roll(x, m, 1)

    def pack(block):
        top, bottom = block[:h], block[h:]
        return (
            jnp.where(first_half, top, turn(bottom)),
            jnp.where(first_half, turn(top), bottom),
        )

    def unpack(low, high):
        return (
            jnp.where(first_half, low, turn(high)),
            jnp.where(first_half, turn(low), high),
        )

    def send_strips(phase, layer, part, low, high, low_side):
        sendx[phase, layer, low_side, part] = low
        sendx[phase, layer, 1 - low_side, part] = high

    def start_strips(phase, layer):
        for side in (0, 1):
            send("tx", side, sendx.at[phase, layer, side], recvx.at[phase, layer, side], slot_of(2 * phase + 1, layer, side))

    def wait_strips(phase, layer):
        for side in (0, 1):
            arrive("tx", side, sendx.at[phase, layer, side], recvx.at[phase, layer, side], slot_of(2 * phase + 1, layer, side))

    def send_columns(phase, layer):
        for part in (0, 1):
            low, high = pack(tile[layer, part, :, own])
            send_strips(phase, layer, part, low, high, 0)
        start_strips(phase, layer)

    def place_columns(phase, layer):
        wait_strips(phase, layer)
        for part in (0, 1):
            top, bottom = unpack(recvx[phase, layer, 0, part], recvx[phase, layer, 1, part])
            tile[layer, part, pl.ds(0, h), other] = top
            tile[layer, part, pl.ds(h, h), other] = bottom

    def send_gradient(phase, layer, g):
        for part in (0, 1):
            grad[layer, part, pl.ds(0, n)] = g[part][:, :core]
            low, high = pack(g[part][:, core:])
            send_strips(phase, layer, part, low, high, 1)
        start_strips(phase, layer)

    def sum_columns(phase, layer):
        wait_strips(phase, layer)
        for part in (0, 1):
            top, bottom = unpack(recvx[phase, layer, 1, part], recvx[phase, layer, 0, part])
            top = grad[layer, part, pl.ds(0, h)] + top
            rim[phase, layer, part, pl.ds(0, h)] = top
            rim[phase, layer, part, pl.ds(h, h)] = grad[layer, part, pl.ds(h, h)] + bottom
            rim[phase, layer, part, pl.ds(n, m)] = top[:m]

    def middle_rows(layer):
        return (
            (rim.at[1, layer, :, pl.ds(core + m, 2 * m), :], recvy.at[layer, 0]),
            (rim.at[1, layer, :, pl.ds(core - m, 2 * m), :], recvy.at[layer, 1]),
        )

    def last_rows(layer):
        return (
            (rim.at[3, layer, :, pl.ds(core + m, m), :], recvl.at[layer, 0]),
            (rim.at[3, layer, :, pl.ds(core, m), :], recvl.at[layer, 1]),
        )

    def send_rows(rows, phase, layer):
        for side in (0, 1):
            src, dst = rows(layer)[side]
            send("ty", side, src, dst, slot_of(phase, layer, side))

    def wait_rows(rows, phase, layer):
        for side in (0, 1):
            src, dst = rows(layer)[side]
            arrive("ty", side, src, dst, slot_of(phase, layer, side))

    def update_middle(layer):
        wait_rows(middle_rows, 2, layer)
        for part in (0, 1):
            for start, side, at in ((0, 1, m), (m, 0, 0), (2 * m, 0, m), (3 * m, 1, 0)):
                rows = pl.ds(start, m)
                total = rim[1, layer, part, rows] + recvy[layer, side, part, pl.ds(at, m)]
                tile[layer, part, rows, own] = tile[layer, part, rows, own] - step_size * total

        @pl.when(ty == 0)
        def _():
            tile[layer, :, before, own] = jnp.zeros((2, m, core), jnp.float32)

        @pl.when(ty == ny - 1)
        def _():
            tile[layer, :, after, own] = jnp.zeros((2, m, core), jnp.float32)

    def update_last(layer):
        wait_rows(last_rows, 4, layer)
        for part in (0, 1):
            for start, side in ((0, 1), (m, 0)):
                rows = pl.ds(start, m)
                total = rim[3, layer, part, rows] + recvl[layer, side, part]
                out_ref[layer, part, rows] = tile[layer, part, rows, own] - step_size * total

    row = lax.broadcasted_iota(jnp.int32, (n, n), 0)
    col = lax.broadcasted_iota(jnp.int32, (n, n), 1)

    def ones(mask):
        return jnp.where(mask, 1.0, 0.0).astype(jnp.bfloat16)

    def pick(left, x, right):
        a, b, c = split3(x)
        y = dot(left, a) + dot(left, b) + dot(left, c)
        a, b, c = split3(y)
        return dot(a, right) + dot(b, right) + dot(c, right)

    def rolled(i, j, shift):
        d = i - j + (m - shift + n)
        return ones((d == 0) | (d == n) | (d == 2 * n))

    roll_rows = rolled(row, col, pos_ref[0, 0, 0, 0])
    roll_cols = rolled(col, row, pos_ref[0, 0, 0, 1])
    for part in (0, 1):
        lit[part] = pick(roll_rows, probe_ref[part], roll_cols)

    def sorted_by_parity(i, j):
        return ones(jnp.where(i < h, 2 * i, 2 * i - n + 1) == j)

    by_row, by_col = sorted_by_parity(row, col), sorted_by_parity(col, row)
    pat[...] = pick(by_row, pat_ref[...], by_col)
    sine, cosine = sin_cos(pick(by_row, phase_ref[...], by_col))
    hk[0] = cosine
    hk[1] = sine

    EVEN, EVEN_T, ODD, ODD_T = 0, 2, 4, 6

    def from_left(table, x):
        high, low = tab_ref[table], tab_ref[table + 1]
        xh, xl = split2(x)
        return dot(cat([high, high, low], 1), cat([xh, xl, xh], 0))

    def from_right(x, table):
        high, low = tab_ref[table], tab_ref[table + 1]
        xh, xl = split2(x)
        return dot(cat([xh, xl, xh], 1), cat([high, high, low], 0))

    def through(field, weigh):
        re, im = field
        even = from_left(EVEN, cat([re[:h] + re[h:], im[:h] + im[h:]], 0))
        odd = from_left(ODD, cat([re[:h] - re[h:], im[:h] - im[h:]], 0))
        re = cat([even[:h], odd[:h]], 0)
        im = cat([even[h:], odd[h:]], 0)
        even = from_right(cat([re[:, :h] + re[:, h:], im[:, :h] + im[:, h:]], 1), EVEN_T)
        odd = from_right(cat([re[:, :h] - re[:, h:], im[:, :h] - im[:, h:]], 1), ODD_T)
        even = cat(weigh((even[:, :h], even[:, h:]), pl.ds(0, h)), 1)
        odd = cat(weigh((odd[:, :h], odd[:, h:]), pl.ds(h, h)), 1)
        even = from_right(even, EVEN)
        odd = from_right(odd, ODD)
        first, second = even + odd, even - odd
        re = cat([first[:, :h], second[:, :h]], 1)
        im = cat([first[:, h:], second[:, h:]], 1)
        even = from_left(EVEN_T, cat([re[:h], im[:h]], 0))
        odd = from_left(ODD_T, cat([re[h:], im[h:]], 0))
        first, second = even + odd, even - odd
        return cat([first[:h], second[:h]], 0), cat([first[h:], second[h:]], 0)

    def forward_kernel(f, cols):
        return cmul((hk[0, :, cols], hk[1, :, cols]), f)

    def backward_kernel(f, cols):
        return cmul_conj((hk[0, :, cols], hk[1, :, cols]), f)

    def residue(f, cols):
        g = f[0] * f[0] + f[1] * f[1] - pat[:, cols]
        return g * f[0], g * f[1]

    def pair(ref, *at):
        return (ref[(*at, 0)], ref[(*at, 1)])

    def entering(layer):
        return pair(lit) if layer == 0 else pair(wave, layer - 1)

    for layer in range(slices):
        for side in (0, 1):
            src, dst = rim_rows(layer)[side]
            arrive("ty", side, src, dst, slot_of(0, layer, side))
        send_columns(0, layer)

    for step in range(STEPS):
        columns, strips = 2 * step, 2 * step + 1
        last = step == STEPS - 1
        rows, phase = (last_rows, 4) if last else (middle_rows, 2)
        for layer in range(slices - 1):
            place_columns(columns, layer)
            moved = through(cmul(entering(layer), pair(tile, layer)), forward_kernel)
            wave[layer, 0] = moved[0]
            wave[layer, 1] = moved[1]
        layer = slices - 1
        place_columns(columns, layer)
        up = through(cmul(entering(layer), pair(tile, layer)), residue)
        for layer in range(slices - 1, -1, -1):
            send_gradient(strips, layer, cmul_conj(entering(layer), up))
            if layer < slices - 1:
                sum_columns(strips, layer + 1)
                send_rows(rows, phase, layer + 1)
            if layer > 0:
                up = through(cmul_conj(pair(tile, layer), up), backward_kernel)
        sum_columns(strips, 0)
        send_rows(rows, phase, 0)
        for layer in range(slices - 1, -1, -1):
            if last:
                update_last(layer)
            else:
                update_middle(layer)
                send_columns(columns + 2, layer)

    for axis, side, src, dst, slot in pending:
        @pl.when(near[axis][side][0])
        def _():
            copy_of(axis, side, src, dst, slot).wait_send()


def shards(object_field, probe, propagator_phase, patterns, scan_positions):
    slices, _, core, _ = object_field.shape
    n = probe.shape[1]
    m = (n - core) // 2
    f32 = jnp.float32
    tables = jnp.asarray(dft_tables(n))
    vmem = pl.BlockSpec(memory_space=pltpu.VMEM)
    slots = 8 * slices * 2
    return pl.pallas_call(
        kernel,
        out_shape=jax.ShapeDtypeStruct(object_field.shape, f32),
        in_specs=[pl.BlockSpec(memory_space=pltpu.SMEM)] + [vmem] * 5,
        out_specs=vmem,
        scratch_shapes=[
            pltpu.VMEM((slices, 2, n, n), f32),
            pltpu.VMEM((2, n, n), f32),
            pltpu.VMEM((2, n, n), f32),
            pltpu.VMEM((n, n), f32),
            pltpu.VMEM((slices - 1, 2, n, n), f32),
            pltpu.VMEM((slices, 2, n, core), f32),
            pltpu.VMEM((2 * STEPS, slices, 2, n + m, core), f32),
            pltpu.VMEM((2 * STEPS, slices, 2, 2, n // 2, core), f32),
            pltpu.VMEM((2 * STEPS, slices, 2, 2, n // 2, core), f32),
            pltpu.VMEM((slices, 2, 2, 2 * m, core), f32),
            pltpu.VMEM((slices, 2, 2, m, core), f32),
            pltpu.SemaphoreType.DMA((slots,)),
            pltpu.SemaphoreType.DMA((slots,)),
        ],
        compiler_params=pltpu.CompilerParams(
            collective_id=0, has_side_effects=True, vmem_limit_bytes=48 * 1024 * 1024
        ),
        name="steps",
    )(scan_positions, object_field, probe, propagator_phase, patterns[0, 0, 0], tables)


def solution(mesh):
    placed = (
        P(None, None, "ty", "tx"),
        P(),
        P(),
        P("ty", "tx", None, None, None),
        P("ty", "tx", None, None),
    )
    return jax.shard_map(
        shards, mesh=mesh, in_specs=placed, out_specs=P(None, None, "ty", "tx"), check_vma=False
    )
```

profile of v0, /device:TPU:6, one launch (start us, length us, event | category | flops | bytes accessed | tf_op | source)
XLA Modules:
  0.0 67.7 jit_solution(8640201817736281932)
XLA Ops:
  0.0 0.0 copy-start.5
  0.0 0.7 copy-done.5
  0.7 0.0 copy-start
  0.7 1.2 %copy-done = bf16[8,256,256]{2,1,0:T(8,128)(2,1)S(1)} copy-done((bf16[8,256,256]{2,1,0:T(8,128)(2,1)S(1)}, bf16[8,256,256]{2,1,0:T(8,128)(2,1)}, u32[]{:S(2)}) %copy-start) | copy-done | bytes 1048600
  1.9 0.0 copy-start.1
  1.9 1.0 %copy-done.1 = f32[2,256,256]{2,1,0:T(8,128)S(1)} copy-done((f32[2,256,256]{2,1,0:T(8,128)S(1)}, f32[2,256,256]{2,1,0:T(8,128)}, u32[]{:S(2)}) %copy-start.1) | copy-done | bytes 524312
  2.9 0.0 copy-start.2
  2.9 1.0 %copy-done.2 = f32[3,2,128,128]{3,2,1,0:T(8,128)S(1)} copy-done((f32[3,2,128,128]{3,2,1,0:T(8,128)S(1)}, f32[3,2,128,128]{3,2,1,0:T(8,128)}, u32[]{:S(2)}) %copy-start.2) | copy-done | bytes 393240
  3.9 0.0 copy-start.3
  3.9 0.9 %copy-done.3 = f32[256,256]{1,0:T(8,128)S(1)} copy-done((f32[256,256]{1,0:T(8,128)S(1)}, f32[256,256]{1,0:T(8,128)}, u32[]{:S(2)}) %copy-start.3) | copy-done | bytes 262168
  4.9 0.0 copy-start.4
  4.9 0.9 %copy-done.4 = f32[1,1,1,256,256]{4,3,2,1,0:T(8,128)S(1)} copy-done((f32[1,1,1,256,256]{4,3,2,1,0:T(8,128)S(1)}, f32[1,1,1,256,256]{4,3,2,1,0:T(8,128)}, u32[]{:S(2)}) %copy-start.4) | copy-done | bytes 262168
  5.8 61.2 %steps.1 = f32[3,2,128,128]{3,2,1,0:T(8,128)S(1)} custom-call(s32[1,1,1,2]{3,2,1,0:T(1,128)S(1)} %copy-done.5, f32[3,2,128,128]{3,2,1,0:T(8,128)S(1)} %copy-done.2, f32[2,256,256]{2,1,0:T(8,128)S(1)} %copy-done.1, f32[256,256]{1,0:T(8,128)S(1)} %copy-done.3, f32[256,256]{1,0:T(8,128)S(1)} %bitcast.1, bf16[8,256,256]{2,1,0:T(8,128)(2,1)S(1)} %copy-done), custom_call_target="tpu_custom_call" | custom-call | tf_op jit(solution)/shard_map/steps/pallas_call | solution.py:399
  67.0 0.7 %copy.8 = f32[3,2,128,128]{3,2,1,0:T(8,128)} copy(f32[3,2,128,128]{3,2,1,0:T(8,128)S(1)} %steps.1) | data formatting | bytes 786432
Async XLA Ops:
  0.0 0.7 copy-start.5
  0.7 1.2 %copy-start = (bf16[8,256,256]{2,1,0:T(8,128)(2,1)S(1)}, bf16[8,256,256]{2,1,0:T(8,128)(2,1)}, u32[]{:S(2)}) copy-start(bf16[8,256,256]{2,1,0:T(8,128)(2,1)} %constant.2.clone.tab_ref) | copy-start | bytes 3145732
  1.9 1.0 %copy-start.1 = (f32[2,256,256]{2,1,0:T(8,128)S(1)}, f32[2,256,256]{2,1,0:T(8,128)}, u32[]{:S(2)}) copy-start(f32[2,256,256]{2,1,0:T(8,128)} %probe_ref.1) | copy-start | bytes 1572868
  2.9 1.0 %copy-start.2 = (f32[3,2,128,128]{3,2,1,0:T(8,128)S(1)}, f32[3,2,128,128]{3,2,1,0:T(8,128)}, u32[]{:S(2)}) copy-start(f32[3,2,128,128]{3,2,1,0:T(8,128)} %obj_ref.1) | copy-start | bytes 1179652
  3.9 0.9 %copy-start.3 = (f32[256,256]{1,0:T(8,128)S(1)}, f32[256,256]{1,0:T(8,128)}, u32[]{:S(2)}) copy-start(f32[256,256]{1,0:T(8,128)} %phase_ref.1) | copy-start | bytes 786436
  4.9 0.9 %copy-start.4 = (f32[1,1,1,256,256]{4,3,2,1,0:T(8,128)S(1)}, f32[1,1,1,256,256]{4,3,2,1,0:T(8,128)}, u32[]{:S(2)}) copy-start(f32[1,1,1,256,256]{4,3,2,1,0:T(8,128)} %param.9) | copy-start | bytes 786436
where the time goes:
time: 68.1 us; the launch traced here: 67.7 us
  Pallas kernels  61.2 us (90%)
  local copies, waits for them, and re-layouts  6.56 us (10%)
    pallas_call x1, Pallas kernels, shards(): pl.pallas_call(kernel, out_shape=jax.ShapeDtypeStruct(object_field.shape,...  61.2 us
    unnamed x13, local copies, waits for them, and re-layouts  6.56 us

commit v1 on v0

--- a/solution.py
+++ b/solution.py
@@ -76,9 +76,9 @@
 
 
 def kernel(
-    pos_ref, obj_ref, probe_ref, phase_ref, pat_ref, tab_ref, out_ref,
+    pos_ref, obj_ref, probe_hbm, phase_hbm, pat_hbm, tab_hbm, out_ref,
     tile, lit, hk, pat, wave, grad, rim, sendx, recvx, recvy, recvl,
-    sem_s, sem_r,
+    probe_ref, tab_ref, sem_s, sem_r, sem_in,
 ):
     slices = obj_ref.shape[0]
     core = obj_ref.shape[2]
@@ -115,6 +115,19 @@
     def slot_of(phase, layer, side):
         return (phase * slices + layer) * 2 + side
 
+    fetch_core, fetch_probe, fetch_phase, fetch_pat, fetch_tab = (
+        pltpu.make_async_copy(src, dst, sem_in.at[i])
+        for i, (src, dst) in enumerate((
+            (obj_ref, tile.at[:, :, pl.ds(0, core), pl.ds(0, core)]),
+            (probe_hbm, probe_ref),
+            (phase_hbm, hk.at[0]),
+            (pat_hbm.at[0, 0, 0], pat),
+            (tab_hbm, tab_ref),
+        ))
+    )
+    for fetch in (fetch_core, fetch_probe, fetch_phase, fetch_pat, fetch_tab):
+        fetch.start()
+
     barrier = pltpu.get_barrier_semaphore()
     count = jnp.int32(0)
     for axis in ("ty", "tx"):
@@ -141,8 +154,6 @@
             src, dst = rim_rows(layer)[side]
             send("ty", side, src, dst, slot_of(0, layer, side))
 
-    tile[:, :, own, own] = obj_ref[...]
-
     @pl.when(ty == 0)
     def _():
         tile[:, :, before, own] = jnp.zeros((slices, 2, m, core), jnp.float32)
@@ -224,10 +235,10 @@
             rim[phase, layer, part, pl.ds(h, h)] = grad[layer, part, pl.ds(h, h)] + bottom
             rim[phase, layer, part, pl.ds(n, m)] = top[:m]
 
-    def middle_rows(layer):
+    def middle_rows(layer, part):
         return (
-            (rim.at[1, layer, :, pl.ds(core + m, 2 * m), :], recvy.at[layer, 0]),
-            (rim.at[1, layer, :, pl.ds(core - m, 2 * m), :], recvy.at[layer, 1]),
+            (rim.at[1, layer, part, pl.ds(core + m, 2 * m), :], recvy.at[layer, 0, part]),
+            (rim.at[1, layer, part, pl.ds(core - m, 2 * m), :], recvy.at[layer, 1, part]),
         )
 
     def last_rows(layer):
@@ -236,19 +247,21 @@
             (rim.at[3, layer, :, pl.ds(core, m), :], recvl.at[layer, 1]),
         )
 
-    def send_rows(rows, phase, layer):
-        for side in (0, 1):
-            src, dst = rows(layer)[side]
-            send("ty", side, src, dst, slot_of(phase, layer, side))
-
-    def wait_rows(rows, phase, layer):
-        for side in (0, 1):
-            src, dst = rows(layer)[side]
-            arrive("ty", side, src, dst, slot_of(phase, layer, side))
+    def send_middle(layer, part):
+        for side in (0, 1):
+            src, dst = middle_rows(layer, part)[side]
+            send("ty", side, src, dst, slot_of((2, 6)[part], layer, side))
+
+    def send_last(layer):
+        for side in (0, 1):
+            src, dst = last_rows(layer)[side]
+            send("ty", side, src, dst, slot_of(4, layer, side))
 
     def update_middle(layer):
-        wait_rows(middle_rows, 2, layer)
-        for part in (0, 1):
+        for part in (0, 1):
+            for side in (0, 1):
+                src, dst = middle_rows(layer, part)[side]
+                arrive("ty", side, src, dst, slot_of((2, 6)[part], layer, side))
             for start, side, at in ((0, 1, m), (m, 0, 0), (2 * m, 0, m), (3 * m, 1, 0)):
                 rows = pl.ds(start, m)
                 total = rim[1, layer, part, rows] + recvy[layer, side, part, pl.ds(at, m)]
@@ -263,7 +276,9 @@
             tile[layer, :, after, own] = jnp.zeros((2, m, core), jnp.float32)
 
     def update_last(layer):
-        wait_rows(last_rows, 4, layer)
+        for side in (0, 1):
+            src, dst = last_rows(layer)[side]
+            arrive("ty", side, src, dst, slot_of(4, layer, side))
         for part in (0, 1):
             for start, side in ((0, 1), (m, 0)):
                 rows = pl.ds(start, m)
@@ -286,19 +301,24 @@
         d = i - j + (m - shift + n)
         return ones((d == 0) | (d == n) | (d == 2 * n))
 
-    roll_rows = rolled(row, col, pos_ref[0, 0, 0, 0])
-    roll_cols = rolled(col, row, pos_ref[0, 0, 0, 1])
-    for part in (0, 1):
-        lit[part] = pick(roll_rows, probe_ref[part], roll_cols)
-
     def sorted_by_parity(i, j):
         return ones(jnp.where(i < h, 2 * i, 2 * i - n + 1) == j)
 
-    by_row, by_col = sorted_by_parity(row, col), sorted_by_parity(col, row)
-    pat[...] = pick(by_row, pat_ref[...], by_col)
-    sine, cosine = sin_cos(pick(by_row, phase_ref[...], by_col))
-    hk[0] = cosine
-    hk[1] = sine
+    def prepare_probe():
+        fetch_probe.wait()
+        roll_rows = rolled(row, col, pos_ref[0, 0, 0, 0])
+        roll_cols = rolled(col, row, pos_ref[0, 0, 0, 1])
+        for part in (0, 1):
+            lit[part] = pick(roll_rows, probe_ref[part], roll_cols)
+
+    def prepare_frequencies():
+        by_row, by_col = sorted_by_parity(row, col), sorted_by_parity(col, row)
+        fetch_phase.wait()
+        sine, cosine = sin_cos(pick(by_row, hk[0], by_col))
+        hk[0] = cosine
+        hk[1] = sine
+        fetch_pat.wait()
+        pat[...] = pick(by_row, pat[...], by_col)
 
     EVEN, EVEN_T, ODD, ODD_T = 0, 2, 4, 6
 
@@ -348,39 +368,57 @@
     def entering(layer):
         return pair(lit) if layer == 0 else pair(wave, layer - 1)
 
-    for layer in range(slices):
+    def first_columns(layer):
         for side in (0, 1):
             src, dst = rim_rows(layer)[side]
             arrive("ty", side, src, dst, slot_of(0, layer, side))
         send_columns(0, layer)
 
+    def next_columns(layer):
+        update_middle(layer)
+        send_columns(2, layer)
+
+    top = slices - 1
+    prepare_probe()
+    fetch_core.wait()
+    first_columns(0)
+    prepare_frequencies()
+    fetch_tab.wait()
     for step in range(STEPS):
         columns, strips = 2 * step, 2 * step + 1
-        last = step == STEPS - 1
-        rows, phase = (last_rows, 4) if last else (middle_rows, 2)
-        for layer in range(slices - 1):
+        bring = first_columns if step == 0 else next_columns
+        if step > 0:
+            bring(0)
+        bring(1)
+        for layer in range(top):
             place_columns(columns, layer)
             moved = through(cmul(entering(layer), pair(tile, layer)), forward_kernel)
             wave[layer, 0] = moved[0]
             wave[layer, 1] = moved[1]
-        layer = slices - 1
-        place_columns(columns, layer)
-        up = through(cmul(entering(layer), pair(tile, layer)), residue)
-        for layer in range(slices - 1, -1, -1):
+            if layer + 2 <= top:
+                bring(layer + 2)
+        place_columns(columns, top)
+        up = through(cmul(entering(top), pair(tile, top)), residue)
+        last = step == STEPS - 1
+        for layer in range(top, -1, -1):
             send_gradient(strips, layer, cmul_conj(entering(layer), up))
-            if layer < slices - 1:
+            if layer < top:
                 sum_columns(strips, layer + 1)
-                send_rows(rows, phase, layer + 1)
+                if last:
+                    send_last(layer + 1)
+                else:
+                    send_middle(layer + 1, 0)
             if layer > 0:
                 up = through(cmul_conj(pair(tile, layer), up), backward_kernel)
         sum_columns(strips, 0)
-        send_rows(rows, phase, 0)
-        for layer in range(slices - 1, -1, -1):
-            if last:
-                update_last(layer)
-            else:
-                update_middle(layer)
-                send_columns(columns + 2, layer)
+        if last:
+            send_last(0)
+        else:
+            send_middle(0, 0)
+            for layer in range(slices):
+                send_middle(layer, 1)
+    for layer in range(top, -1, -1):
+        update_last(layer)
 
     for axis, side, src, dst, slot in pending:
         @pl.when(near[axis][side][0])
@@ -395,11 +433,12 @@
     f32 = jnp.float32
     tables = jnp.asarray(dft_tables(n))
     vmem = pl.BlockSpec(memory_space=pltpu.VMEM)
+    hbm = pl.BlockSpec(memory_space=pltpu.HBM)
     slots = 8 * slices * 2
     return pl.pallas_call(
         kernel,
         out_shape=jax.ShapeDtypeStruct(object_field.shape, f32),
-        in_specs=[pl.BlockSpec(memory_space=pltpu.SMEM)] + [vmem] * 5,
+        in_specs=[pl.BlockSpec(memory_space=pltpu.SMEM)] + [hbm] * 5,
         out_specs=vmem,
         scratch_shapes=[
             pltpu.VMEM((slices, 2, n, n), f32),
@@ -413,14 +452,17 @@
             pltpu.VMEM((2 * STEPS, slices, 2, 2, n // 2, core), f32),
             pltpu.VMEM((slices, 2, 2, 2 * m, core), f32),
             pltpu.VMEM((slices, 2, 2, m, core), f32),
+            pltpu.VMEM((2, n, n), f32),
+            pltpu.VMEM(tables.shape, jnp.bfloat16),
             pltpu.SemaphoreType.DMA((slots,)),
             pltpu.SemaphoreType.DMA((slots,)),
+            pltpu.SemaphoreType.DMA((5,)),
         ],
         compiler_params=pltpu.CompilerParams(
-            collective_id=0, has_side_effects=True, vmem_limit_bytes=48 * 1024 * 1024
+            collective_id=0, has_side_effects=True, vmem_limit_bytes=63 * 1024 * 1024
         ),
         name="steps",
-    )(scan_positions, object_field, probe, propagator_phase, patterns[0, 0, 0], tables)
+    )(scan_positions, object_field, probe, propagator_phase, patterns, tables)
 
 
 def solution(mesh):

time: 68.1 us -> 66.2 us (0.972)
  local copies, waits for them, and re-layouts: 6.56 us -> 1.77 us
  Pallas kernels: 61.2 us -> 63.7 us
    unnamed x13 -> x1, local copies, waits for them, and re-layouts: 6.56 us -> 1.77 us
    pallas_call x1, Pallas kernels: 61.2 us -> 63.7 us  [shards(): pl.pallas_call(kernel, out_shape=jax.ShapeDtypeStruct(object_field.shape,...]
where the time goes in v1:
time: 66.2 us; the launch traced here: 65.5 us
  Pallas kernels  63.7 us (96%)
  local copies, waits for them, and re-layouts  1.77 us (3%)
    pallas_call x1, Pallas kernels, shards(): pl.pallas_call(kernel, out_shape=jax.ShapeDtypeStruct(object_field.shape,...  63.7 us
    unnamed x1, local copies, waits for them, and re-layouts  1.77 us

profile of v1, /device:TPU:6, one launch (start us, length us, event | category | flops | bytes accessed | tf_op | source)
XLA Modules:
  0.0 65.5 jit_solution(1901668588997814705)
XLA Ops:
  0.0 63.7 %steps.1 = f32[3,2,128,128]{3,2,1,0:T(8,128)} custom-call(s32[1,1,1,2]{3,2,1,0:T(1,128)} %pos_ref.1, f32[3,2,128,128]{3,2,1,0:T(8,128)} %obj_ref.1, f32[2,256,256]{2,1,0:T(8,128)} %probe_hbm.1, f32[256,256]{1,0:T(8,128)} %phase_hbm.1, f32[1,1,1,256,256]{4,3,2,1,0:T(8,128)} %pat_hbm.1, bf16[8,256,256]{2,1,0:T(8,128)(2,1)} %constant.2.clone.tab_hbm), custom_call_target="tpu_custom_call" | custom-call | tf_op jit(solution)/shard_map/steps/pallas_call | solution.py:438
  63.7 1.8 %copy.8 = f32[3,2,128,128]{3,2,1,0:T(8,128)} copy(f32[3,2,128,128]{3,2,1,0:T(8,128)} %steps.1) | data formatting | bytes 786432

commit v2 on v1

--- a/solution.py
+++ b/solution.py
@@ -78,7 +78,7 @@
 def kernel(
     pos_ref, obj_ref, probe_hbm, phase_hbm, pat_hbm, tab_hbm, out_ref,
     tile, lit, hk, pat, wave, grad, rim, sendx, recvx, recvy, recvl,
-    probe_ref, tab_ref, sem_s, sem_r, sem_in,
+    probe_ref, tab_ref, field, sem_s, sem_r, sem_in,
 ):
     slices = obj_ref.shape[0]
     core = obj_ref.shape[2]
@@ -91,7 +91,7 @@
         "ty": ((ty > 0, (ty - 1, tx)), (ty < ny - 1, (ty + 1, tx))),
         "tx": ((tx > 0, (ty, tx - 1)), (tx < nx - 1, (ty, tx + 1))),
     }
-    pending = []
+    pending = {}
 
     def copy_of(axis, side, src, dst, slot):
         return pltpu.make_async_remote_copy(
@@ -100,12 +100,12 @@
             device_id=near[axis][side][1], device_id_type=pl.DeviceIdType.MESH,
         )
 
-    def send(axis, side, src, dst, slot):
+    def send(axis, side, ends, slot):
         @pl.when(near[axis][side][0])
         def _():
-            copy_of(axis, side, src, dst, slot).start()
-
-        pending.append((axis, side, src, dst, slot))
+            copy_of(axis, side, *ends(), slot).start()
+
+        pending[slot] = (axis, side, ends)
 
     def arrive(axis, side, src, dst, slot):
         @pl.when(near[axis][1 - side][0])
@@ -149,10 +149,11 @@
             (obj_ref.at[layer, :, tail, :], tile.at[layer, :, before, own]),
         )
 
-    for layer in range(slices):
-        for side in (0, 1):
-            src, dst = rim_rows(layer)[side]
-            send("ty", side, src, dst, slot_of(0, layer, side))
+    def send_rim(layer):
+        for side in (0, 1):
+            send("ty", side, lambda side=side: rim_rows(layer)[side], slot_of(0, layer, side))
+
+    send_rim(0)
 
     @pl.when(ty == 0)
     def _():
@@ -200,7 +201,10 @@
 
     def start_strips(phase, layer):
         for side in (0, 1):
-            send("tx", side, sendx.at[phase, layer, side], recvx.at[phase, layer, side], slot_of(2 * phase + 1, layer, side))
+            send(
+                "tx", side, lambda side=side: (sendx.at[phase, layer, side], recvx.at[phase, layer, side]),
+                slot_of(2 * phase + 1, layer, side),
+            )
 
     def wait_strips(phase, layer):
         for side in (0, 1):
@@ -249,19 +253,19 @@
 
     def send_middle(layer, part):
         for side in (0, 1):
-            src, dst = middle_rows(layer, part)[side]
-            send("ty", side, src, dst, slot_of((2, 6)[part], layer, side))
+            send("ty", side, lambda side=side: middle_rows(layer, part)[side], slot_of((2, 6)[part], layer, side))
 
     def send_last(layer):
         for side in (0, 1):
-            src, dst = last_rows(layer)[side]
-            send("ty", side, src, dst, slot_of(4, layer, side))
+            send("ty", side, lambda side=side: last_rows(layer)[side], slot_of(4, layer, side))
 
     def update_middle(layer):
         for part in (0, 1):
             for side in (0, 1):
                 src, dst = middle_rows(layer, part)[side]
                 arrive("ty", side, src, dst, slot_of((2, 6)[part], layer, side))
+            if part == 0 and layer + 1 < slices:
+                send_middle(layer + 1, 1)
             for start, side, at in ((0, 1, m), (m, 0, 0), (2 * m, 0, m), (3 * m, 1, 0)):
                 rows = pl.ds(start, m)
                 total = rim[1, layer, part, rows] + recvy[layer, side, part, pl.ds(at, m)]
@@ -332,8 +336,15 @@
         xh, xl = split2(x)
         return dot(cat([xh, xl, xh], 1), cat([high, high, low], 0))
 
-    def through(field, weigh):
-        re, im = field
+    def through(stage):
+        at_top = stage == slices - 1
+        sign = jnp.where(at_top, 0.0, jnp.where(stage < slices - 1, 1.0, -1.0)).astype(jnp.float32)
+
+        def weigh(f, cols):
+            power = f[0] * f[0] + f[1] * f[1] - pat[:, cols]
+            return cmul((jnp.where(at_top, power, hk[0, :, cols]), sign * hk[1, :, cols]), f)
+
+        re, im = field[0], field[1]
         even = from_left(EVEN, cat([re[:h] + re[h:], im[:h] + im[h:]], 0))
         odd = from_left(ODD, cat([re[:h] - re[h:], im[:h] - im[h:]], 0))
         re = cat([even[:h], odd[:h]], 0)
@@ -350,17 +361,8 @@
         even = from_left(EVEN_T, cat([re[:h], im[:h]], 0))
         odd = from_left(ODD_T, cat([re[h:], im[h:]], 0))
         first, second = even + odd, even - odd
-        return cat([first[:h], second[:h]], 0), cat([first[h:], second[h:]], 0)
-
-    def forward_kernel(f, cols):
-        return cmul((hk[0, :, cols], hk[1, :, cols]), f)
-
-    def backward_kernel(f, cols):
-        return cmul_conj((hk[0, :, cols], hk[1, :, cols]), f)
-
-    def residue(f, cols):
-        g = f[0] * f[0] + f[1] * f[1] - pat[:, cols]
-        return g * f[0], g * f[1]
+        field[0] = cat([first[:h], second[:h]], 0)
+        field[1] = cat([first[h:], second[h:]], 0)
 
     def pair(ref, *at):
         return (ref[(*at, 0)], ref[(*at, 1)])
@@ -379,51 +381,68 @@
         send_columns(2, layer)
 
     top = slices - 1
+    stages = 2 * slices - 1
+
+    def put(value):
+        field[0] = value[0]
+        field[1] = value[1]
+
+    def ahead(step, stage):
+        if stage <= top:
+            if stage == 0 and step > 0:
+                next_columns(0)
+            if stage == 0:
+                (next_columns if step else first_columns)(1)
+            place_columns(2 * step, stage)
+            put(cmul(entering(stage), pair(tile, stage)))
+        else:
+            put(cmul_conj(pair(tile, 2 * top - stage + 1), pair(field)))
+
+    def behind(step, stage):
+        last = step == STEPS - 1
+        if stage < top:
+            wave[stage] = field[...]
+            if stage + 2 <= top:
+                (next_columns if step else first_columns)(stage + 2)
+            return
+        layer = 2 * top - stage
+        send_gradient(2 * step + 1, layer, cmul_conj(entering(layer), pair(field)))
+        for done in ([layer + 1] if layer < top else []) + ([0] if layer == 0 else []):
+            sum_columns(2 * step + 1, done)
+            if last:
+                send_last(done)
+            else:
+                send_middle(done, 0)
+        if layer == 0 and not last:
+            send_middle(0, 1)
+
     prepare_probe()
     fetch_core.wait()
+    send_rim(1)
     first_columns(0)
+    for layer in range(2, slices):
+        send_rim(layer)
     prepare_frequencies()
     fetch_tab.wait()
-    for step in range(STEPS):
-        columns, strips = 2 * step, 2 * step + 1
-        bring = first_columns if step == 0 else next_columns
-        if step > 0:
-            bring(0)
-        bring(1)
-        for layer in range(top):
-            place_columns(columns, layer)
-            moved = through(cmul(entering(layer), pair(tile, layer)), forward_kernel)
-            wave[layer, 0] = moved[0]
-            wave[layer, 1] = moved[1]
-            if layer + 2 <= top:
-                bring(layer + 2)
-        place_columns(columns, top)
-        up = through(cmul(entering(top), pair(tile, top)), residue)
-        last = step == STEPS - 1
-        for layer in range(top, -1, -1):
-            send_gradient(strips, layer, cmul_conj(entering(layer), up))
-            if layer < top:
-                sum_columns(strips, layer + 1)
-                if last:
-                    send_last(layer + 1)
-                else:
-                    send_middle(layer + 1, 0)
-            if layer > 0:
-                up = through(cmul_conj(pair(tile, layer), up), backward_kernel)
-        sum_columns(strips, 0)
-        if last:
-            send_last(0)
-        else:
-            send_middle(0, 0)
-            for layer in range(slices):
-                send_middle(layer, 1)
+
+    def turn_of(i, carry):
+        for step in range(STEPS):
+            for stage in range(stages):
+                pl.when(i == step * stages + stage)(functools.partial(ahead, step, stage))
+        through(lax.rem(i, stages))
+        for step in range(STEPS):
+            for stage in range(stages):
+                pl.when(i == step * stages + stage)(functools.partial(behind, step, stage))
+        return carry
+
+    lax.fori_loop(0, STEPS * stages, turn_of, 0)
     for layer in range(top, -1, -1):
         update_last(layer)
 
-    for axis, side, src, dst, slot in pending:
+    for slot, (axis, side, ends) in pending.items():
         @pl.when(near[axis][side][0])
         def _():
-            copy_of(axis, side, src, dst, slot).wait_send()
+            copy_of(axis, side, *ends(), slot).wait_send()
 
 
 def shards(object_field, probe, propagator_phase, patterns, scan_positions):
@@ -454,6 +473,7 @@
             pltpu.VMEM((slices, 2, 2, m, core), f32),
             pltpu.VMEM((2, n, n), f32),
             pltpu.VMEM(tables.shape, jnp.bfloat16),
+            pltpu.VMEM((2, n, n), f32),
             pltpu.SemaphoreType.DMA((slots,)),
             pltpu.SemaphoreType.DMA((slots,)),
             pltpu.SemaphoreType.DMA((5,)),

time: 66.2 us -> 65.7 us (level)
  no operation moved by 1% of the time
where the time goes in v2:
time: 65.7 us; the launch traced here: 65.5 us
  Pallas kernels  63.8 us (97%)
  local copies, waits for them, and re-layouts  1.77 us (3%)
    pallas_call x1, Pallas kernels, shards(): pl.pallas_call(kernel, out_shape=jax.ShapeDtypeStruct(object_field.shape,...  63.8 us
    unnamed x1, local copies, waits for them, and re-layouts  1.77 us

profile of v2, /device:TPU:6, one launch (start us, length us, event | category | flops | bytes accessed | tf_op | source)
XLA Modules:
  0.0 65.5 jit_solution(15113521402654189844)
XLA Ops:
  0.0 63.8 %steps.1 = f32[3,2,128,128]{3,2,1,0:T(8,128)} custom-call(s32[1,1,1,2]{3,2,1,0:T(1,128)} %pos_ref.1, f32[3,2,128,128]{3,2,1,0:T(8,128)} %obj_ref.1, f32[2,256,256]{2,1,0:T(8,128)} %probe_hbm.1, f32[256,256]{1,0:T(8,128)} %phase_hbm.1, f32[1,1,1,256,256]{4,3,2,1,0:T(8,128)} %pat_hbm.1, bf16[8,256,256]{2,1,0:T(8,128)(2,1)} %constant.2.clone.tab_hbm), custom_call_target="tpu_custom_call" | custom-call | tf_op jit(solution)/shard_map/steps/pallas_call | solution.py:457
  63.8 1.8 %copy.8 = f32[3,2,128,128]{3,2,1,0:T(8,128)} copy(f32[3,2,128,128]{3,2,1,0:T(8,128)} %steps.1) | data formatting | bytes 786432

commit v3 on v2

--- a/solution.py
+++ b/solution.py
@@ -329,12 +329,14 @@
     def from_left(table, x):
         high, low = tab_ref[table], tab_ref[table + 1]
         xh, xl = split2(x)
-        return dot(cat([high, high, low], 1), cat([xh, xl, xh], 0))
+        both = dot(cat([high, low], 0), xh)
+        return both[:n] + (both[n:] + dot(high, xl))
 
     def from_right(x, table):
         high, low = tab_ref[table], tab_ref[table + 1]
         xh, xl = split2(x)
-        return dot(cat([xh, xl, xh], 1), cat([high, high, low], 0))
+        both = dot(cat([xh, xl], 0), high)
+        return both[:n] + (both[n:] + dot(xh, low))
 
     def through(stage):
         at_top = stage == slices - 1

time: 65.7 us -> 65.6 us (level)
  no operation moved by 1% of the time
where the time goes in v3:
time: 65.6 us; the launch traced here: 65.5 us
  Pallas kernels  63.7 us (97%)
  local copies, waits for them, and re-layouts  1.77 us (3%)
    pallas_call x1, Pallas kernels, shards(): pl.pallas_call(kernel, out_shape=jax.ShapeDtypeStruct(object_field.shape,...  63.7 us
    unnamed x1, local copies, waits for them, and re-layouts  1.77 us

profile of v3, /device:TPU:6, one launch (start us, length us, event | category | flops | bytes accessed | tf_op | source)
XLA Modules:
  0.0 65.5 jit_solution(10801170472896016602)
XLA Ops:
  0.0 63.7 %steps.1 = f32[3,2,128,128]{3,2,1,0:T(8,128)} custom-call(s32[1,1,1,2]{3,2,1,0:T(1,128)} %pos_ref.1, f32[3,2,128,128]{3,2,1,0:T(8,128)} %obj_ref.1, f32[2,256,256]{2,1,0:T(8,128)} %probe_hbm.1, f32[256,256]{1,0:T(8,128)} %phase_hbm.1, f32[1,1,1,256,256]{4,3,2,1,0:T(8,128)} %pat_hbm.1, bf16[8,256,256]{2,1,0:T(8,128)(2,1)} %constant.2.clone.tab_hbm), custom_call_target="tpu_custom_call" | custom-call | tf_op jit(solution)/shard_map/steps/pallas_call | solution.py:459
  63.7 1.8 %copy.8 = f32[3,2,128,128]{3,2,1,0:T(8,128)} copy(f32[3,2,128,128]{3,2,1,0:T(8,128)} %steps.1) | data formatting | bytes 786432
